TPU v7x, 32 devices: a whole 2x2x4 slice. The times are simulated.
32 devices in a mesh: blk: 8 (over z, y), tp: 4 (over x, core).
Axes of the slice: x: 2, y: 2, z: 4, core: 2. Of those that a mesh axis runs over, the one named last changes fastest.
Arguments:
- queries: bfloat16 [8192, 1664], P(('blk', 'tp')), may hold values from -120 to 120
- keys: bfloat16 [8192, 1664], P(('blk', 'tp')), may hold values from -6 to 6
- values: bfloat16 [8192, 1664], P(('blk', 'tp')), may hold values from -6 to 6
- segment_ids: int32 [8192], replicated, may hold values from -1 to 7, as said below
- proj_weight: bfloat16 [6656, 3072], P(None, 'tp'), may hold values from -0.078125 to 0.078125
Outputs:
- normed: bfloat16 [2048, 3072], P('blk', 'tp')
- seg_peaks: float32 [8], replicated
Inputs may be any that keep to these rules, and one draw needn't show every extreme that they name: `segment_ids`: ids other than -1 never fall along the pack; every image 0 to 7 occurs as one run of tokens that starts at a multiple of 4 and has a multiple of 4 tokens, at most 1024; some image has exactly 1024; -1 marks padding tokens, which may stand between images.
All inputs are finite; a program needn't handle non-finite values.
Results may differ from a plain program's by a relative error of at most 0.0056.
Values may be sent and summed in bfloat16 or wider, within the bound.
A program may use at most 128 MiB of HBM per device.

v0:
```python
import jax
import jax.numpy as jnp
from jax import lax
from jax.sharding import PartitionSpec as P

HEAD = 128


masked_score = -1e30
epsilon = 1e-06


def from_behind(x, axis, by):
    devices = lax.axis_size(axis)
    pairs = [(i, i + by) for i in range(devices) if 0 <= i + by < devices]
    return lax.ppermute(x, axis, pairs)


def key_scores(query_heads, key_heads):
    return jnp.einsum(
        "rhd,khd->hrk", query_heads, key_heads, preferred_element_type=jnp.float32
    ) * HEAD ** (-0.5)


def finish(scores, allowed, value_heads):
    scores = jnp.where(allowed[None], scores, masked_score)
    row_top = jnp.max(scores, axis=2, keepdims=True)
    exp_terms = jnp.where(allowed[None], jnp.exp(scores - row_top), 0.0)
    row_total = jnp.maximum(jnp.sum(exp_terms, axis=2), 1.0)
    weights = exp_terms.astype(jnp.bfloat16)
    mixed_out = jnp.einsum("hrk,khd->rhd", weights, value_heads, preferred_element_type=jnp.float32)
    return mixed_out / row_total.T[:, :, None]


def per_device(queries, keys, values, segment_ids, proj_weight):
    group_count = lax.axis_size("blk")
    group_index = lax.axis_index("blk")
    part_index = lax.axis_index("tp")
    row_count = queries.shape[0]
    width = queries.shape[1]
    heads_count = width // HEAD
    block_len = segment_ids.shape[0] // group_count
    own_begin = group_index * block_len
    query_segs = lax.dynamic_slice_in_dim(
        segment_ids, own_begin + part_index * row_count, row_count
    )
    own_keys, own_values = (
        lax.all_gather(keys, "tp", axis=0, tiled=True),
        lax.all_gather(values, "tp", axis=0, tiled=True),
    )
    before_keys, before_values = from_behind((own_keys, own_values), "blk", 1)
    after_keys, after_values = from_behind((own_keys, own_values), "blk", -1)

    def neighbor_segs(offset):
        target = group_index + offset
        inside = (target >= 0) & (target < group_count)
        begin_at = jnp.clip(target, 0, group_count - 1) * block_len
        return jnp.where(inside, lax.dynamic_slice_in_dim(segment_ids, begin_at, block_len), -2)

    seg_sets = (neighbor_segs(-1), neighbor_segs(0), neighbor_segs(1))
    key_sets = (before_keys, own_keys, after_keys)
    masks = [
        (query_segs[:, None] == key_segs[None, :]) & (query_segs[:, None] >= 0)
        for key_segs in seg_sets
    ]
    query_heads = queries.reshape(row_count, heads_count, HEAD)
    all_keys = jnp.concatenate(key_sets, axis=0).reshape(3 * block_len, heads_count, HEAD)
    scores = key_scores(query_heads, all_keys)
    full_mask = jnp.concatenate(masks, axis=1)
    value_heads = jnp.concatenate((before_values, own_values, after_values), axis=0).reshape(
        3 * block_len, heads_count, HEAD
    )
    attended = finish(scores, full_mask, value_heads).reshape(row_count, width).astype(jnp.bfloat16)
    merged = attended.reshape(row_count // 4, 4 * width)
    projected = jnp.dot(
        lax.all_gather(merged, "tp", axis=0, tiled=True),
        proj_weight,
        preferred_element_type=jnp.float32,
    )
    row_segs = lax.dynamic_slice_in_dim(segment_ids, own_begin, block_len)[::4]
    member = row_segs[:, None] == jnp.arange(group_count, dtype=jnp.int32)[None, :]
    squares = jnp.sum(projected * projected, axis=1)
    seg_sums = jnp.sum(jnp.where(member, squares[:, None], 0.0), axis=0)
    seg_counts = jnp.sum(member.astype(jnp.float32), axis=0) * projected.shape[1]
    row_peak = jnp.max(jnp.where(member, jnp.max(projected, axis=1)[:, None], masked_score), axis=0)
    seg_sums, seg_counts = lax.psum((seg_sums, seg_counts), ("blk", "tp"))
    row_peak = lax.pmax(row_peak, ("blk", "tp"))
    seg_scale = lax.rsqrt(seg_sums / seg_counts + epsilon)
    row_scale = jnp.sum(jnp.where(member, seg_scale[None, :], 0.0), axis=1)
    normed = (projected * row_scale[:, None]).astype(jnp.bfloat16)
    return (normed, row_peak * seg_scale)


def solution(mesh):
    in_specs = (
        P(("blk", "tp"), None),
        P(("blk", "tp"), None),
        P(("blk", "tp"), None),
        P(),
        P(None, "tp"),
    )
    out_specs = (P("blk", "tp"), P())
    return jax.shard_map(
        per_device, mesh=mesh, in_specs=in_specs, out_specs=out_specs, check_vma=False
    )
```

profile of v0, /device:TPU:0, one launch (start us, length us, event | category | flops | bytes accessed | tf_op | source)
XLA Modules:
  0.0 512.0 jit_solution(16878866346115660055)
XLA Ops:
  7.2 2.2 copy.18
  10.2 32.5 %all-gather.6.cloned.1.call-done = bf16[1024,1664]{0,1:T(8,128)(2,1)} async-done(((bf16[256,1664]{0,1:T(8,128)(2,1)}), bf16[1024,1664]{0,1:T(8,128)(2,1)}) %all-gather.6.cloned.1.call-update) | async-done | bytes 3407888 | tf_op jit(solution)/shard_map/all_gather | solution.py:48
  42.7 3.6 collective-permute-start.2
  46.3 1.3 collective-permute-start.3
  47.7 2.2 copy.19
  51.5 0.8 compare_and_fusion.2
  52.3 1.2 pad_add_fusion
  53.5 20.9 %all-gather.4.cloned.1.call-done = bf16[1024,1664]{1,0:T(8,128)(2,1)} async-done(((bf16[256,1664]{1,0:T(8,128)(2,1)}), bf16[1024,1664]{1,0:T(8,128)(2,1)}) %all-gather.4.cloned.1.call-update) | async-done | bytes 3407888 | tf_op jit(solution)/shard_map/all_gather | solution.py:49
  74.4 5.1 collective-permute-start
  79.5 1.3 collective-permute-start.1
  80.7 185.8 %collective-permute-done.2 = bf16[1024,1664]{0,1:T(8,128)(2,1)S(1)} collective-permute-done((bf16[1024,1664]{0,1:T(8,128)(2,1)}, bf16[1024,1664]{0,1:T(8,128)(2,1)S(1)}, u32[]{:S(2)}, u32[]{:S(2)}) %collective-permute-start.2) | collective-permute-done | bytes 3407904 | tf_op jit(solution)/shard_map/ppermute | solution.py:16
  266.5 8.1 %pad_maximum_fusion.1 = bf16[3072,1664]{0,1:T(8,128)(2,1)} fusion(bf16[1024,1664]{0,1:T(8,128)(2,1)} %collective-permute-done.3, bf16[1024,1664]{0,1:T(8,128)(2,1)} %all-gather.6.cloned.1.call-done, bf16[1024,1664]{0,1:T(8,128)(2,1)S(1)} %collective-permute-done.2), kind=kLoop, calls=%fused_computation.10 | loop fusion | flops 30670848 | bytes 20447232 | tf_op jit(solution)/shard_map/concatenate | solution.py:67
  274.7 29.4 %fusion.16 = (f32[13,256]{1,0:T(8,128)S(1)}, bf16[13,256,3072]{1,2,0:T(8,128)(2,1)}) fusion(pred[256,3072]{0,1:T(8,128)(4,1)} %pad_add_fusion, bf16[3072,13,128]{0,2,1:T(8,128)(2,1)} %bitcast.22, bf16[256,13,128]{0,2,1:T(8,128)(2,1)} %bitcast.24), kind=kOutput, calls=%fused_computation.36 | convolution fusion | flops 2678590464 | bytes 32322560 | tf_op jit(solution)/shard_map/sub | solution.py:28
  304.1 34.8 %collective-permute-done = bf16[1024,1664]{1,0:T(8,128)(2,1)} collective-permute-done((bf16[1024,1664]{1,0:T(8,128)(2,1)}, bf16[1024,1664]{1,0:T(8,128)(2,1)}, u32[]{:S(2)}, u32[]{:S(2)}) %collective-permute-start) | collective-permute-done | bytes 3407904 | tf_op jit(solution)/shard_map/ppermute | solution.py:16
  338.9 15.9 %pad_maximum_fusion = bf16[3072,1664]{1,0:T(8,128)(2,1)} fusion(bf16[1024,1664]{1,0:T(8,128)(2,1)} %collective-permute-done.1, bf16[1024,1664]{1,0:T(8,128)(2,1)S(1)} %copy-done, bf16[1024,1664]{1,0:T(8,128)(2,1)} %collective-permute-done), kind=kLoop, calls=%fused_computation.9 | loop fusion | flops 30670848 | bytes 20447232 | tf_op jit(solution)/shard_map/concatenate | solution.py:70
  354.8 14.3 %copy.17 = bf16[3072,1664]{0,1:T(8,128)(2,1)} copy(bf16[3072,1664]{1,0:T(8,128)(2,1)} %pad_maximum_fusion) | data formatting | bytes 20447232 | tf_op jit(solution)/shard_map/concatenate | solution.py:70
  369.1 12.5 %fusion.7 = bf16[256,13,128]{0,2,1:T(8,128)(2,1)S(1)} fusion(bf16[3072,13,128]{0,2,1:T(8,128)(2,1)} %bitcast.23, bf16[13,256,3072]{1,2,0:T(8,128)(2,1)} %get-tuple-element.20, f32[256,13]{0,1:T(8,128)S(1)} %maximum_bitcast_fusion), kind=kOutput, calls=%fused_computation.13 | convolution fusion | flops 2618097664 | bytes 31536128 | tf_op jit(solution)/shard_map/hrk,khd->rhd/dot_general | solution.py:31
  381.6 1.2 copy.23
  382.9 1.5 convert_element_type.18
  384.6 30.9 %all-gather.8.cloned.1.call-done = bf16[256,6656]{1,0:T(8,128)(2,1)} async-done(((bf16[64,6656]{1,0:T(8,128)(2,1)}), bf16[256,6656]{1,0:T(8,128)(2,1)}) %all-gather.8.cloned.1.call-update) | async-done | bytes 3407888 | tf_op jit(solution)/shard_map/all_gather | solution.py:76
  415.6 7.9 %fusion.14 = (f32[256]{0:T(256)S(1)}, f32[256]{0:T(256)S(1)}, f32[256,768]{1,0:T(8,128)S(1)}) fusion(bf16[256,6656]{1,0:T(8,128)(2,1)} %all-gather.8.cloned.1.call-done, bf16[6656,768]{1,0:T(8,128)(2,1)} %param.9), kind=kOutput, calls=%fused_computation.34 | convolution fusion | flops 2617835008 | bytes 14419968 | tf_op jit(solution)/shard_map/dot_general | solution.py:75
  423.6 39.4 %all-reduce = (f32[8]{0:T(128)S(1)}, f32[8]{0:T(128)S(1)}) all-reduce(f32[8]{0:T(128)S(1)} %get-tuple-element.7, f32[8]{0:T(128)S(1)} %broadcast_multiply_fusion), channel_id=1, replica_groups=mesh['blk'=8,'tp'=4] {'blk','tp'}, use_global_device_ids=true, to_apply=%region_4.5 | all-reduce | flops 16 | bytes 128 | tf_op jit(solution)/shard_map/psum | solution.py:86
  463.1 41.0 %pmax.7 = f32[8]{0:T(128)S(1)} all-reduce(f32[8]{0:T(128)S(1)} %get-tuple-element.4), channel_id=1, replica_groups=mesh['blk'=8,'tp'=4] {'blk','tp'}, use_global_device_ids=true, to_apply=%region_10.11 | all-reduce | flops 8 | bytes 64 | tf_op jit(solution)/shard_map/pmax | solution.py:87
  504.6 0.9 multiply_convert_fusion
  (19 shorter events, 3.5 us)
Async XLA Ops:
  7.2 35.6 %all-gather.6.cloned.1.call-start = ((), (), s32[]{:S(2)}) async-start(), calls=%async_computation.1 | async-start | bytes 4259840 | tf_op jit(solution)/shard_map/all_gather | solution.py:48
  9.4 64.9 %all-gather.4.cloned.1.call-start = ((), (), s32[]{:S(2)}) async-start(), calls=%async_computation | async-start | bytes 4259840 | tf_op jit(solution)/shard_map/all_gather | solution.py:49
  10.2 405.4 %all-gather.8.cloned.1.call-start = ((), (), s32[]{:S(2)}) async-start(), calls=%async_computation.2 | async-start | bytes 4259840 | tf_op jit(solution)/shard_map/all_gather | solution.py:76
  42.7 223.8 %collective-permute-start.2 = (bf16[1024,1664]{0,1:T(8,128)(2,1)}, bf16[1024,1664]{0,1:T(8,128)(2,1)S(1)}, u32[]{:S(2)}, u32[]{:S(2)}) collective-permute-start(bf16[1024,1664]{0,1:T(8,128)(2,1)} %all-gather.6.cloned.1.call-done), channel_id=1, source_target_pairs={{0,4},{4,8},{8,12},{12,16},{16,20},{20,24},{24,28},{1,5},{5,9},{9,... | collective-permute-start | bytes 10223624 | tf_op jit(solution)/shard_map/ppermute | solution.py:16
  46.3 220.2 %collective-permute-start.3 = (bf16[1024,1664]{0,1:T(8,128)(2,1)}, bf16[1024,1664]{0,1:T(8,128)(2,1)}, u32[]{:S(2)}, u32[]{:S(2)}) collective-permute-start(bf16[1024,1664]{0,1:T(8,128)(2,1)} %all-gather.6.cloned.1.call-done), channel_id=1, source_target_pairs={{4,0},{8,4},{12,8},{16,12},{20,16},{24,20},{28,24},{5,1},{9,5},{13... | collective-permute-start | bytes 10223624 | tf_op jit(solution)/shard_map/ppermute | solution.py:16
  74.4 264.5 %collective-permute-start = (bf16[1024,1664]{1,0:T(8,128)(2,1)}, bf16[1024,1664]{1,0:T(8,128)(2,1)}, u32[]{:S(2)}, u32[]{:S(2)}) collective-permute-start(bf16[1024,1664]{1,0:T(8,128)(2,1)} %all-gather.4.cloned.1.call-done), channel_id=1, source_target_pairs={{0,4},{4,8},{8,12},{12,16},{16,20},{20,24},{24,28},{1,5},{5,9},{9,... | collective-permute-start | bytes 10223624 | tf_op jit(solution)/shard_map/ppermute | solution.py:16
  79.5 259.5 %collective-permute-start.1 = (bf16[1024,1664]{1,0:T(8,128)(2,1)}, bf16[1024,1664]{1,0:T(8,128)(2,1)}, u32[]{:S(2)}, u32[]{:S(2)}) collective-permute-start(bf16[1024,1664]{1,0:T(8,128)(2,1)} %all-gather.4.cloned.1.call-done), channel_id=1, source_target_pairs={{4,0},{8,4},{12,8},{16,12},{20,16},{24,20},{28,24},{5,1},{9,5},{13... | collective-permute-start | bytes 10223624 | tf_op jit(solution)/shard_map/ppermute | solution.py:16
  274.6 64.3 %copy-start = (bf16[1024,1664]{1,0:T(8,128)(2,1)S(1)}, bf16[1024,1664]{1,0:T(8,128)(2,1)}, u32[]{:S(2)}) copy-start(bf16[1024,1664]{1,0:T(8,128)(2,1)} %all-gather.4.cloned.1.call-done) | copy-start | bytes 10223620
Sparse Core Ops, SparseCore 0:
  9.6 33.1 all-gather.5
  44.3 30.0 all-gather.3
  384.5 30.9 all-gather.7
where the time goes:
time: 513 us; the launch traced here: 512 us
  waiting for transfers between devices  306 us (60%)
  blocking collectives  80.4 us (16%)
  matrix products  49.8 us (10%)
  other arithmetic  29.2 us (6%)
  local copies, waits for them, and re-layouts  21.7 us (4%)
  between operations  13.8 us (3%)
  starting transfers between devices  11.4 us (2%)
    ppermute x4, waiting for transfers between devices, from_behind(): return lax.ppermute(x, axis, pairs)  221 us
    pmax x1, blocking collectives, per_device(): row_peak = lax.pmax(row_peak, ('blk', 'tp'))  41 us
    psum x1, blocking collectives, per_device(): seg_sums, seg_counts = lax.psum((seg_sums, seg_counts), ('blk', 'tp'))  39.4 us
    all_gather x1, waiting for transfers between devices, per_device(): lax.all_gather(keys, 'tp', axis=0, tiled=True)  32.5 us
    all_gather x1, waiting for transfers between devices, per_device(): lax.all_gather(merged, 'tp', axis=0, tiled=True)  30.9 us
    sub x1, matrix products, finish(): exp_terms = jnp.where(allowed[None], jnp.exp(scores - row_top), 0.0)  29.4 us
    all_gather x1, waiting for transfers between devices, per_device(): lax.all_gather(values, 'tp', axis=0, tiled=True)  20.9 us
    concatenate x1, other arithmetic, per_device(): jnp.concatenate((before_values, own_values, after_values), axis=0)  15.9 us
  transfers between devices with their start and end apart: 7, of which 5 were waited for; matrix products, arithmetic and copies ran while one was open for 9% of the time, Pallas kernels for 0%

commit v1 on v0

v1 whole, which is shorter than its diff:
```python
import functools

import jax
import jax.numpy as jnp
from jax import lax
from jax.experimental import pallas as pl
from jax.experimental.pallas import tpu as pltpu
from jax.sharding import PartitionSpec as P

HEAD = 128
MERGE = 4
QUERY_TILE = 256
KEY_TILE = 512
LANES = 128
masked_score = -1e30
least_top = -1e20
epsilon = 1e-06
score_scale = HEAD ** (-0.5) * 1.4426950408889634
MESH = pl.DeviceIdType.MESH


def start_head(place, places, heads):
    return (place * heads) // places


def exchange_kernel(
    tp, pairs, heads, slots, block_len,
    q_ref, k_ref, v_ref, qg_ref, kg_ref, vg_ref,
    send, recv, pass_send, pass_recv, own_sem,
):
    blk, part = lax.axis_index("blk"), lax.axis_index("tp")
    side, pair = lax.rem(blk, 2), blk // 2
    places = 2 * tp
    place = side * tp + part
    rows = q_ref.shape[0]
    offsets = [(dy, dt) for dy in (1, 0) for dt in range(tp) if (dy, dt) != (0, 0)]
    arrays = ((k_ref, kg_ref, block_len), (v_ref, vg_ref, block_len), (q_ref, qg_ref, 0))
    has_prev, has_next = pair > 0, pair < pairs - 1
    n_around = jnp.minimum(pair, 1) + jnp.minimum(pairs - 1 - pair, 1)

    barrier = pltpu.get_barrier_semaphore()
    for dy, dt in offsets:
        target = (pair * 2 + lax.rem(side + dy, 2), lax.rem(part + dt, tp))
        pl.semaphore_signal(barrier, inc=1, device_id=target, device_id_type=MESH)

    @pl.when(has_prev)
    def _():
        pl.semaphore_signal(barrier, inc=1, device_id=(blk - 2, part), device_id_type=MESH)

    @pl.when(has_next)
    def _():
        pl.semaphore_signal(barrier, inc=1, device_id=(blk + 2, part), device_id_type=MESH)

    pl.semaphore_wait(barrier, len(offsets) + n_around)

    def push(a, i):
        src, dst, first = arrays[a]
        dy, dt = offsets[i]
        to_side, to_part = lax.rem(side + dy, 2), lax.rem(part + dt, tp)
        column = start_head(to_side * tp + to_part, places, heads) * HEAD
        return pltpu.make_async_remote_copy(
            src_ref=src.at[:, pl.ds(pl.multiple_of(column, HEAD), slots * HEAD)],
            dst_ref=dst.at[pl.ds(pl.multiple_of(first + place * rows, rows), rows), :],
            send_sem=send.at[a, i],
            recv_sem=recv.at[a, i],
            device_id=(pair * 2 + to_side, to_part),
            device_id_type=MESH,
        )

    def keep(a):
        src, dst, first = arrays[a]
        column = start_head(place, places, heads) * HEAD
        return pltpu.make_async_copy(
            src.at[:, pl.ds(pl.multiple_of(column, HEAD), slots * HEAD)],
            dst.at[pl.ds(pl.multiple_of(first + place * rows, rows), rows), :],
            own_sem.at[a],
        )

    def hand_on(a, forward):
        dst = arrays[a][1]
        if forward:
            src_rows, dst_rows, target = pl.ds(2 * block_len, block_len), pl.ds(0, block_len), blk + 2
        else:
            src_rows, dst_rows, target = pl.ds(block_len, block_len), pl.ds(3 * block_len, block_len), blk - 2
        return pltpu.make_async_remote_copy(
            src_ref=dst.at[src_rows, :],
            dst_ref=dst.at[dst_rows, :],
            send_sem=pass_send.at[a, forward],
            recv_sem=pass_recv.at[a, forward],
            device_id=(target, part),
            device_id_type=MESH,
        )

    def start_all(a):
        for i in range(len(offsets)):
            push(a, i).start()
        keep(a).start()

    def arrive_all(a):
        for i in range(len(offsets)):
            push(a, i).wait_recv()
        keep(a).wait()

    def hand_on_all(a):
        @pl.when(has_prev)
        def _():
            hand_on(a, 0).start()

        @pl.when(has_next)
        def _():
            hand_on(a, 1).start()

    start_all(0)
    start_all(1)
    arrive_all(0)
    hand_on_all(0)
    start_all(2)
    arrive_all(1)
    hand_on_all(1)
    arrive_all(2)
    for a in range(3):
        for i in range(len(offsets)):
            push(a, i).wait_send()
    for a in range(2):
        @pl.when(has_prev)
        def _(a=a):
            hand_on(a, 0).wait_send()
            hand_on(a, 1).wait_recv()

        @pl.when(has_next)
        def _(a=a):
            hand_on(a, 1).wait_send()
            hand_on(a, 0).wait_recv()


def attend_kernel(slots, low_ref, high_ref, q_ref, k_ref, v_ref, qs_ref, ks_ref, o_ref, mixed_ref):
    tile = pl.program_id(0)
    query_segs = qs_ref[...]
    rows = q_ref.shape[0]

    def step(chunk, carry):
        at = pl.ds(pl.multiple_of(chunk * KEY_TILE, KEY_TILE), KEY_TILE)
        same = query_segs == ks_ref[:, at]
        after = []
        for slot in range(slots):
            top, total, mixed = carry[slot]
            columns = slice(slot * HEAD, (slot + 1) * HEAD)
            scores = lax.dot_general(
                q_ref[:, columns], k_ref[at, columns], (((1,), (1,)), ((), ())),
                preferred_element_type=jnp.float32,
            )
            scores = jnp.where(same, scores, masked_score)
            new_top = jnp.maximum(top, jnp.max(scores, axis=1, keepdims=True))
            terms = jnp.exp2((scores - new_top) * score_scale)
            decay = jnp.exp2((top - new_top) * score_scale)
            total = total * decay + jnp.sum(terms, axis=1, keepdims=True)
            mixed = mixed * decay + jnp.dot(
                terms.astype(jnp.bfloat16), v_ref[at, columns], preferred_element_type=jnp.float32
            )
            after.append((new_top, total, mixed))
        return tuple(after)

    begin = tuple(
        (
            jnp.full((rows, 1), least_top, jnp.float32),
            jnp.zeros((rows, 1), jnp.float32),
            jnp.zeros((rows, HEAD), jnp.float32),
        )
        for _ in range(slots)
    )
    final = lax.fori_loop(low_ref[tile], high_ref[tile], step, begin)
    for slot in range(slots):
        _, total, mixed = final[slot]
        mixed_ref[slot] = mixed / jnp.maximum(total, 1.0)
    for slot in range(slots):
        for r in range(MERGE):
            o_ref[slot, 0, r] = mixed_ref[slot, pl.ds(r, rows // MERGE, stride=MERGE), :].astype(jnp.bfloat16)


def project_kernel(
    tp, blks, heads, slots,
    o_ref, w_ref, seg_ref, count_ref, normed_ref, peak_ref,
    merged, weight, projected, part_stats, blk_stats,
    w_sem, own_sem, y_send, y_recv, x_send, x_recv, c_send, c_recv, f_send, f_recv,
    p_send, p_recv, b_send, b_recv,
):
    blk, part = lax.axis_index("blk"), lax.axis_index("tp")
    side, place_x, core = lax.rem(blk, 2), part // 2, lax.rem(part, 2)
    x_len, places = tp // 2, 2 * tp
    here = (blk, part)
    sibling = (blk, part + 1 - 2 * core)
    across = (blk + 1 - 2 * side, part)
    load = pltpu.make_async_copy(w_ref, weight, w_sem)
    load.start()

    barrier = pltpu.get_barrier_semaphore()
    for d in range(1, tp):
        pl.semaphore_signal(barrier, inc=1, device_id=(blk, lax.rem(part + d, tp)), device_id_type=MESH)
    for d in range(1, blks):
        pl.semaphore_signal(barrier, inc=1, device_id=(lax.rem(blk + d, blks), part), device_id_type=MESH)
    pl.semaphore_wait(barrier, tp + blks - 2)

    def first(place):
        return start_head(place, places, heads)

    def held(place, slot):
        return slot < first(place + 1) - first(place)

    def place_of(kind, to_x, to_core):
        return (side if kind == 0 else 1 - side) * tp + to_x * 2 + to_core

    def copy(src, head, send_sem, recv_sem, target):
        return pltpu.make_async_remote_copy(
            src_ref=src, dst_ref=merged.at[head], send_sem=send_sem, recv_sem=recv_sem,
            device_id=target, device_id_type=MESH,
        )

    own = place_of(0, place_x, core)
    far = place_of(1, place_x, core)

    def clipped(place, slot):
        return jnp.minimum(first(place) + slot, heads - 1)

    def stay(slot):
        return pltpu.make_async_copy(o_ref.at[slot, side], merged.at[clipped(own, slot)], own_sem.at[slot])

    def go_y(slot):
        return copy(o_ref.at[slot, 1 - side], clipped(own, slot), y_send.at[slot], y_recv.at[slot], across)

    def source(kind, slot):
        return o_ref.at[slot, side] if kind == 0 else merged.at[clipped(far, slot)]

    def go_x(kind, slot, d):
        target = (blk, lax.rem(place_x + d, x_len) * 2 + core)
        head = clipped(own if kind == 0 else far, slot)
        return copy(source(kind, slot), head, x_send.at[kind, slot, d - 1], x_recv.at[kind, slot, d - 1], target)

    def go_c(kind, slot):
        head = clipped(own if kind == 0 else far, slot)
        return copy(source(kind, slot), head, c_send.at[kind, slot], c_recv.at[kind, slot], sibling)

    def go_f(kind, slot, d):
        came = clipped(place_of(kind, lax.rem(place_x + x_len - d, x_len), core), slot)
        return copy(merged.at[came], came, f_send.at[kind, slot, d - 1], f_recv.at[kind, slot, d - 1], sibling)

    slot_range, steps = range(slots), range(1, x_len)

    for slot in slot_range:
        @pl.when(held(own, slot))
        def _(slot=slot):
            go_y(slot).start()
            for d in steps:
                go_x(0, slot, d).start()
            go_c(0, slot).start()
            stay(slot).start()

    for slot in slot_range:
        @pl.when(held(far, slot))
        def _(slot=slot):
            go_y(slot).wait_recv()
            for d in steps:
                go_x(1, slot, d).start()
            go_c(1, slot).start()

    for kind in range(2):
        for d in steps:
            for slot in slot_range:
                @pl.when(held(place_of(kind, lax.rem(place_x + x_len - d, x_len), core), slot))
                def _(kind=kind, d=d, slot=slot):
                    go_x(kind, slot, d).wait_recv()
                    go_f(kind, slot, d).start()

    for slot in slot_range:
        @pl.when(held(own, slot))
        def _(slot=slot):
            stay(slot).wait()
            go_y(slot).wait_send()

        for kind in range(2):
            @pl.when(held(own if kind == 0 else far, slot))
            def _(kind=kind, slot=slot):
                for d in steps:
                    go_x(kind, slot, d).wait_send()
                go_c(kind, slot).wait_send()

            @pl.when(held(place_of(kind, place_x, 1 - core), slot))
            def _(kind=kind, slot=slot):
                go_c(kind, slot).wait_recv()

            for d in steps:
                from_x = lax.rem(place_x + x_len - d, x_len)

                @pl.when(held(place_of(kind, from_x, core), slot))
                def _(kind=kind, slot=slot, d=d):
                    go_f(kind, slot, d).wait_send()

                @pl.when(held(place_of(kind, from_x, 1 - core), slot))
                def _(kind=kind, slot=slot, d=d):
                    go_f(kind, slot, d).wait_recv()
    load.wait()

    rows = projected.shape[0]
    width = heads * HEAD

    def product(r):
        at = pl.ds(pl.multiple_of(r * rows, rows), rows)
        left = jnp.concatenate([merged[h, at, :] for h in range(heads)], axis=1)
        right = weight[pl.ds(pl.multiple_of(r * width, width), width), :]
        return jnp.dot(left, right, preferred_element_type=jnp.float32)

    projected[...] = product(0)

    @pl.loop(1, MERGE)
    def _(r):
        projected[...] += product(r)

    values = projected[...]
    lane = lax.broadcasted_iota(jnp.int32, (rows, LANES), 1)
    member = seg_ref[...] == lane
    squares = jnp.sum(values * values, axis=1, keepdims=True)
    tops = jnp.max(values, axis=1, keepdims=True)
    sums = jnp.sum(jnp.where(member, squares, 0.0), axis=0, keepdims=True)
    peaks = jnp.max(jnp.where(member, tops, masked_score), axis=0, keepdims=True)
    line = lax.broadcasted_iota(jnp.int32, (8, LANES), 0)

    def spread(stats, tile, me, count, target_of, send, recv):
        stats[me] = tile

        def send_to(d):
            return pltpu.make_async_remote_copy(
                src_ref=stats.at[me], dst_ref=stats.at[me],
                send_sem=send.at[d - 1], recv_sem=recv.at[d - 1],
                device_id=target_of(d), device_id_type=MESH,
            )

        for d in range(1, count):
            send_to(d).start()
        for d in range(1, count):
            send_to(d).wait()
        every = stats[...]
        return jnp.where(line == 0, jnp.sum(every, axis=0), jnp.max(every, axis=0))

    tile = jnp.where(line == 0, sums, peaks)
    tile = spread(part_stats, tile, part, tp, lambda d: (blk, lax.rem(part + d, tp)), p_send, p_recv)
    tile = spread(blk_stats, tile, blk, blks, lambda d: (lax.rem(blk + d, blks), part), b_send, b_recv)
    scale = lax.rsqrt(tile[0:1] / jnp.maximum(count_ref[...], 1.0) + epsilon)
    row_scale = jnp.sum(jnp.where(member, scale, 0.0), axis=1, keepdims=True)
    normed_ref[...] = (values * row_scale).astype(jnp.bfloat16)
    peak_ref[...] = jnp.broadcast_to(tile[1:2] * scale, (8, LANES))


def per_device(queries, keys, values, segment_ids, proj_weight):
    blks, tp = lax.axis_size("blk"), lax.axis_size("tp")
    blk = lax.axis_index("blk")
    rows, width = queries.shape
    heads = width // HEAD
    tokens = segment_ids.shape[0]
    block_len = tokens // blks
    pairs, places = blks // 2, 2 * tp
    slots = -(-heads // places)
    peers = places - 1
    pair_len = 2 * block_len
    columns = proj_weight.shape[1]
    dma, anywhere = pltpu.SemaphoreType.DMA, pl.BlockSpec(memory_space=pl.ANY)
    in_vmem = pl.BlockSpec(memory_space=pltpu.VMEM)

    begin = (blk // 2) * pair_len
    edge = jnp.full((block_len,), -2, jnp.int32)
    key_segs = lax.dynamic_slice_in_dim(jnp.concatenate([edge, segment_ids, edge]), begin, 2 * pair_len)
    query_segs = lax.dynamic_slice_in_dim(segment_ids, begin, pair_len)
    tiles = query_segs.reshape(pair_len // QUERY_TILE, QUERY_TILE)
    least = jnp.min(jnp.where(tiles >= 0, tiles, tokens), axis=1)[:, None]
    most = jnp.max(tiles, axis=1)[:, None]
    meets = (key_segs[None] >= least) & (key_segs[None] <= most)
    chunk = jnp.arange(2 * pair_len, dtype=jnp.int32)[None] // KEY_TILE
    low = jnp.min(jnp.where(meets, chunk, 2 * pair_len), axis=1)
    high = jnp.max(jnp.where(meets, chunk + 1, 0), axis=1)
    row_segs = lax.dynamic_slice_in_dim(segment_ids, blk * block_len, block_len)[::MERGE]
    lanes = jnp.arange(LANES, dtype=jnp.int32)
    counts = jnp.sum((segment_ids[::MERGE][:, None] == lanes).astype(jnp.float32), axis=0, keepdims=True)
    counts = counts * (columns * tp)

    held = slots * HEAD
    query_cols, key_cols, value_cols = pl.pallas_call(
        functools.partial(exchange_kernel, tp, pairs, heads, slots, block_len),
        out_shape=[
            jax.ShapeDtypeStruct((pair_len, held), jnp.bfloat16),
            jax.ShapeDtypeStruct((2 * pair_len, held), jnp.bfloat16),
            jax.ShapeDtypeStruct((2 * pair_len, held), jnp.bfloat16),
        ],
        in_specs=[anywhere] * 3,
        out_specs=[anywhere] * 3,
        scratch_shapes=[dma((3, peers)), dma((3, peers)), dma((2, 2)), dma((2, 2)), dma((3,))],
        compiler_params=pltpu.CompilerParams(collective_id=0, has_side_effects=True),
        name="exchange",
    )(queries, keys, values)

    per_block = block_len // QUERY_TILE
    merge_rows = QUERY_TILE // MERGE
    whole = lambda i, low, high: (0, 0)
    by_tile = lambda i, low, high: (i, 0)
    attended = pl.pallas_call(
        functools.partial(attend_kernel, slots),
        out_shape=jax.ShapeDtypeStruct((slots, 2, MERGE, block_len // MERGE, HEAD), jnp.bfloat16),
        grid_spec=pltpu.PrefetchScalarGridSpec(
            num_scalar_prefetch=2,
            grid=(2 * per_block,),
            in_specs=[
                pl.BlockSpec((QUERY_TILE, held), by_tile),
                pl.BlockSpec((2 * pair_len, held), whole),
                pl.BlockSpec((2 * pair_len, held), whole),
                pl.BlockSpec((QUERY_TILE, 1), by_tile),
                pl.BlockSpec((1, 2 * pair_len), whole),
            ],
            out_specs=pl.BlockSpec(
                (slots, 1, MERGE, merge_rows, HEAD),
                lambda i, low, high: (0, i // per_block, 0, i % per_block, 0),
            ),
            scratch_shapes=[pltpu.VMEM((slots, QUERY_TILE, HEAD), jnp.float32)],
        ),
        compiler_params=pltpu.CompilerParams(vmem_limit_bytes=40 * 1024 * 1024),
        name="attend",
    )(
        low, high, query_cols, key_cols, value_cols,
        jnp.where(query_segs >= 0, query_segs, -3)[:, None], key_segs[None],
    )
    attended = attended.reshape(slots, 2, block_len, HEAD)

    x_len = tp // 2
    merged_rows = block_len // MERGE
    sems = [dma(()), dma((slots,)), dma((slots,)), dma((slots,))]
    sems += [dma((2, slots, x_len - 1))] * 2 + [dma((2, slots))] * 2 + [dma((2, slots, x_len - 1))] * 2
    sems += [dma((tp - 1,))] * 2 + [dma((blks - 1,))] * 2
    normed, peaks = pl.pallas_call(
        functools.partial(project_kernel, tp, blks, heads, slots),
        out_shape=[
            jax.ShapeDtypeStruct((merged_rows, columns), jnp.bfloat16),
            jax.ShapeDtypeStruct((8, LANES), jnp.float32),
        ],
        in_specs=[in_vmem, anywhere, in_vmem, in_vmem],
        out_specs=[in_vmem, in_vmem],
        scratch_shapes=[
            pltpu.VMEM((heads, block_len, HEAD), jnp.bfloat16),
            pltpu.VMEM(proj_weight.shape, jnp.bfloat16),
            pltpu.VMEM((merged_rows, columns), jnp.float32),
            pltpu.VMEM((tp, 8, LANES), jnp.float32),
            pltpu.VMEM((blks, 8, LANES), jnp.float32),
        ] + sems,
        compiler_params=pltpu.CompilerParams(
            collective_id=1, has_side_effects=True, vmem_limit_bytes=48 * 1024 * 1024
        ),
        name="project",
    )(attended, proj_weight, row_segs[:, None], counts)
    return normed, peaks[0, :blks]


def solution(mesh):
    in_specs = (
        P(("blk", "tp"), None),
        P(("blk", "tp"), None),
        P(("blk", "tp"), None),
        P(),
        P(None, "tp"),
    )
    out_specs = (P("blk", "tp"), P())
    return jax.shard_map(
        per_device, mesh=mesh, in_specs=in_specs, out_specs=out_specs, check_vma=False
    )
```

time: 513 us -> 112 us (0.22)
  waiting for transfers between devices: 306 us -> 0 us
  Pallas kernels: 0 us -> 102 us
  blocking collectives: 80.4 us -> 0 us
  matrix products: 49.8 us -> 0 us
  other arithmetic: 29.2 us -> 2.21 us
  local copies, waits for them, and re-layouts: 21.7 us -> 8.18 us
  between operations: 13.8 us -> 0.75 us
  starting transfers between devices: 11.4 us -> 0 us
    ppermute x4 -> x0, waiting for transfers between devices: 221 us -> none  [from_behind(): return lax.ppermute(x, axis, pairs)]
    pallas_call x0 -> x3, Pallas kernels: none -> 102 us  [the longest x1 41.8 us: per_device(): pl.pallas_call(functools.partial(exchange_kernel, tp, pairs, heads, slots...]
    all_gather x3 -> x0, waiting for transfers between devices: 84.3 us -> none  [the longest x1 32.5 us: per_device(): lax.all_gather(keys, 'tp', axis=0, tiled=True)]
    pmax x1 -> x0, blocking collectives: 41 us -> none  [per_device(): row_peak = lax.pmax(row_peak, ('blk', 'tp'))]
    psum x1 -> x0, blocking collectives: 39.4 us -> none  [per_device(): seg_sums, seg_counts = lax.psum((seg_sums, seg_counts), ('blk', 'tp'))]
    sub x1 -> x0, matrix products: 29.4 us -> none  [finish(): exp_terms = jnp.where(allowed[None], jnp.exp(scores - row_top), 0.0)]
    concatenate x3 -> x0, other arithmetic: 25.2 us -> none  [the longest x1 15.9 us: per_device(): jnp.concatenate((before_values, own_values, after_values), axis=0)]
    dot_general x2 -> x0, matrix products: 20.4 us -> none  [the longest x1 12.5 us: finish(): jnp.einsum('hrk,khd->rhd', weights, value_heads, preferred_element_type=j...]
  transfers between devices with their start and end apart: 7 -> 0, of which waited for: 5 -> 0; matrix products, arithmetic and copies ran while one was open for 9% -> 0% of each run, Pallas kernels for 0% -> 0%
where the time goes in v1:
time: 112 us; the launch traced here: 113 us
  Pallas kernels  102 us (91%)
  local copies, waits for them, and re-layouts  8.18 us (7%)
  other arithmetic  2.21 us (2%)
    pallas_call x1, Pallas kernels, per_device(): pl.pallas_call(functools.partial(exchange_kernel, tp, pairs, heads, slots...  41.8 us
    pallas_call x1, Pallas kernels, per_device(): pl.pallas_call(functools.partial(project_kernel, tp, blks, heads, slots),...  37 us
    pallas_call x1, Pallas kernels, per_device(): pl.pallas_call(functools.partial(attend_kernel, slots), out_shape=jax.Sha...  22.9 us
    unnamed x7, local copies, waits for them, and re-layouts  5.14 us

profile of v1, /device:TPU:0, one launch (start us, length us, event | category | flops | bytes accessed | tf_op | source)
XLA Modules:
  0.0 112.9 jit_solution(13166123991562056036)
XLA Ops:
  0.6 0.7 compare_select_fusion
  1.4 0.4 copy.9.qs_ref
  1.7 0.1 fusion.5
  1.9 0.7 add_select_fusion
  2.7 0.3 select_reduce_fusion
  2.9 41.8 %exchange.1 = (bf16[2048,256]{1,0:T(8,128)(2,1)}, bf16[4096,256]{1,0:T(8,128)(2,1)}, bf16[4096,256]{1,0:T(8,128)(2,1)}) custom-call(bf16[256,1664]{1,0:T(8,128)(2,1)} %q_ref.1, bf16[256,1664]{1,0:T(8,128)(2,1)} %k_ref.1, bf16[256,1664]{1,0:T(8,128)(2,1)} %v_ref.1), custom_call_target="tpu_custom_call" | custom-call | tf_op jit(solution)/shard_map/exchange/pallas_call | solution.py:384
  44.7 0.0 copy-start
  44.7 1.6 %copy-done = bf16[4096,256]{1,0:T(8,128)(2,1)S(1)} copy-done((bf16[4096,256]{1,0:T(8,128)(2,1)S(1)}, bf16[4096,256]{1,0:T(8,128)(2,1)}, u32[]{:S(2)}) %copy-start) | copy-done | bytes 2097176
  46.3 0.0 copy-start.1
  46.3 1.6 %copy-done.1 = bf16[4096,256]{1,0:T(8,128)(2,1)S(1)} copy-done((bf16[4096,256]{1,0:T(8,128)(2,1)S(1)}, bf16[4096,256]{1,0:T(8,128)(2,1)}, u32[]{:S(2)}) %copy-start.1) | copy-done | bytes 2097176
  47.9 0.0 copy-start.2
  47.9 1.2 %copy-done.2 = bf16[2048,256]{1,0:T(8,128)(2,1)S(1)} copy-done((bf16[2048,256]{1,0:T(8,128)(2,1)S(1)}, bf16[2048,256]{1,0:T(8,128)(2,1)}, u32[]{:S(2)}) %copy-start.2) | copy-done | bytes 1048600
  49.1 22.9 %attend.1 = bf16[2,2,4,256,128]{4,3,2,1,0:T(8,128)(2,1)S(1)} custom-call(s32[8]{0:T(128)S(1)} %get-tuple-element.13.low_ref, s32[8]{0:T(128)S(1)} %get-tuple-element.12.high_ref, bf16[2048,256]{1,0:T(8,128)(2,1)S(1)} %copy-done.2, bf16[4096,256]{1,0:T(8,128)(2,1)S(1)} %copy-done, bf16[4096,256]{1,0:T(8,128)(2,1)S(1)} %copy-done.1, ...), custom_call_target="tpu_custom_call" | custom-call | tf_op jit(solution)/shard_map/attend/pallas_call | solution.py:402
  72.1 0.7 dynamic_slice.11
  72.8 0.2 slice.9
  73.0 0.1 copy.10.seg_ref
  73.1 1.1 slice.10
  74.2 0.4 convert_reduce_fusion
  74.6 37.0 %project.1 = (bf16[256,768]{1,0:T(8,128)(2,1)S(1)}, f32[8,128]{1,0:T(8,128)S(1)}) custom-call(bf16[2,2,1024,128]{3,2,1,0:T(8,128)(2,1)S(1)} %bitcast.8, bf16[6656,768]{1,0:T(8,128)(2,1)} %w_ref.1, s32[256,1]{1,0:T(8,128)S(1)} %copy.10.seg_ref, f32[1,128]{1,0:T(1,128)S(1)} %multiply_bitcast_fusion.count_ref), custom_call_target="tpu_custom_call" | custom-call | tf_op jit(solution)/shard_map/project/pallas_call | solution.py:434
  111.6 0.5 slice_bitcast_fusion
  112.1 0.7 copy.12
  (4 shorter events, 0.0 us)
Async XLA Ops:
  44.7 1.6 %copy-start = (bf16[4096,256]{1,0:T(8,128)(2,1)S(1)}, bf16[4096,256]{1,0:T(8,128)(2,1)}, u32[]{:S(2)}) copy-start(bf16[4096,256]{1,0:T(8,128)(2,1)} %get-tuple-element.8.k_ref) | copy-start | bytes 6291460
  46.3 1.6 %copy-start.1 = (bf16[4096,256]{1,0:T(8,128)(2,1)S(1)}, bf16[4096,256]{1,0:T(8,128)(2,1)}, u32[]{:S(2)}) copy-start(bf16[4096,256]{1,0:T(8,128)(2,1)} %get-tuple-element.9.v_ref) | copy-start | bytes 6291460
  47.9 1.2 %copy-start.2 = (bf16[2048,256]{1,0:T(8,128)(2,1)S(1)}, bf16[2048,256]{1,0:T(8,128)(2,1)}, u32[]{:S(2)}) copy-start(bf16[2048,256]{1,0:T(8,128)(2,1)} %get-tuple-element.7.q_ref) | copy-start | bytes 3145732

commit v2 on v0

v2 whole, which is shorter than its diff:
```python
import functools

import jax
import jax.numpy as jnp
from jax import lax
from jax.experimental import pallas as pl
from jax.experimental.pallas import tpu as pltpu
from jax.sharding import PartitionSpec as P

HEAD = 128
MERGE = 4
QUERY_TILE = 256
KEY_TILE = 768
LANES = 128
masked_score = -1e30
least_top = -1e20
epsilon = 1e-06
score_scale = HEAD ** (-0.5) * 1.4426950408889634
MESH = pl.DeviceIdType.MESH


def start_head(place, places, heads):
    return (place * heads) // places


def whole_kernel(
    tp, blks, heads, slots, block_len,
    q_in, k_in, v_in, seg_ref, w_ref, normed_ref, peak_ref,
    queries, keys, values_held, key_marks, query_marks, o_ref, mixed_ref,
    merged, weight, projected, part_stats, blk_stats,
    send, recv, keep_sem, pass_send, pass_recv,
    w_sem, own_sem, y_send, y_recv, x_send, x_recv, c_send, c_recv, f_send, f_recv,
    p_send, p_recv, b_send, b_recv,
):
    blk, part = lax.axis_index("blk"), lax.axis_index("tp")
    side, place_x, core = lax.rem(blk, 2), part // 2, lax.rem(part, 2)
    pair, pairs = blk // 2, blks // 2
    x_len, places = tp // 2, 2 * tp
    place = side * tp + part
    sibling = (blk, part + 1 - 2 * core)
    across = (blk + 1 - 2 * side, part)
    slab = q_in.shape[0]
    load = pltpu.make_async_copy(w_ref, weight, w_sem)

    barrier = pltpu.get_barrier_semaphore()
    for d in range(1, tp):
        other_part = lax.rem(part + d, tp)
        pl.semaphore_signal(barrier, inc=1, device_id=(blk, other_part), device_id_type=MESH)
        pl.semaphore_signal(barrier, inc=1, device_id=(across[0], other_part), device_id_type=MESH)
    for d in range(1, blks):
        pl.semaphore_signal(barrier, inc=1, device_id=(lax.rem(blk + d, blks), part), device_id_type=MESH)

    has_prev, has_next = pair > 0, pair < pairs - 1

    @pl.when(pair == 0)
    def _():
        for ref in (keys, values_held):
            ref[:, 0:block_len, :] = jnp.zeros((slots, block_len, HEAD), jnp.bfloat16)

    @pl.when(pair == pairs - 1)
    def _():
        for ref in (keys, values_held):
            ref[:, 3 * block_len : 4 * block_len, :] = jnp.zeros((slots, block_len, HEAD), jnp.bfloat16)

    pl.semaphore_wait(barrier, 2 * (tp - 1) + blks - 1)

    def first(place):
        return start_head(place, places, heads)

    def held(place, slot):
        return slot < first(place + 1) - first(place)

    def place_of(kind, to_x, to_core):
        return (side if kind == 0 else 1 - side) * tp + to_x * 2 + to_core

    def copy(src, head, send_sem, recv_sem, target):
        return pltpu.make_async_remote_copy(
            src_ref=src, dst_ref=merged.at[head], send_sem=send_sem, recv_sem=recv_sem,
            device_id=target, device_id_type=MESH,
        )

    own = place_of(0, place_x, core)
    far = place_of(1, place_x, core)

    def clipped(place, slot):
        return jnp.minimum(first(place) + slot, heads - 1)

    def stay(slot):
        return pltpu.make_async_copy(o_ref.at[slot, side], merged.at[clipped(own, slot)], own_sem.at[slot])

    def go_y(slot):
        return copy(o_ref.at[slot, 1 - side], clipped(own, slot), y_send.at[slot], y_recv.at[slot], across)

    def source(kind, slot):
        return o_ref.at[slot, side] if kind == 0 else merged.at[clipped(far, slot)]

    def go_x(kind, slot, d):
        target = (blk, lax.rem(place_x + d, x_len) * 2 + core)
        head = clipped(own if kind == 0 else far, slot)
        return copy(source(kind, slot), head, x_send.at[kind, slot, d - 1], x_recv.at[kind, slot, d - 1], target)

    def go_c(kind, slot):
        head = clipped(own if kind == 0 else far, slot)
        return copy(source(kind, slot), head, c_send.at[kind, slot], c_recv.at[kind, slot], sibling)

    def go_f(kind, slot, d):
        came = clipped(place_of(kind, lax.rem(place_x + x_len - d, x_len), core), slot)
        return copy(merged.at[came], came, f_send.at[kind, slot, d - 1], f_recv.at[kind, slot, d - 1], sibling)

    offsets = [(dy, dt) for dy in (1, 0) for dt in range(tp) if (dy, dt) != (0, 0)]
    arrays = ((k_in, keys, block_len), (v_in, values_held, block_len), (q_in, queries, 0))

    def push(a, slot, i):
        src, dst, base = arrays[a]
        dy, dt = offsets[i]
        to_side, to_part = lax.rem(side + dy, 2), lax.rem(part + dt, tp)
        column = clipped(to_side * tp + to_part, slot) * HEAD
        return pltpu.make_async_remote_copy(
            src_ref=src.at[:, pl.ds(pl.multiple_of(column, HEAD), HEAD)],
            dst_ref=dst.at[slot, pl.ds(pl.multiple_of(base + place * slab, slab), slab), :],
            send_sem=send.at[a, slot, i],
            recv_sem=recv.at[a, slot, i],
            device_id=(pair * 2 + to_side, to_part),
            device_id_type=MESH,
        )

    def pushed_to(slot, i):
        dy, dt = offsets[i]
        return held(lax.rem(side + dy, 2) * tp + lax.rem(part + dt, tp), slot)

    def keep(a, slot):
        src, dst, base = arrays[a]
        return pltpu.make_async_copy(
            src.at[:, pl.ds(pl.multiple_of(clipped(place, slot) * HEAD, HEAD), HEAD)],
            dst.at[slot, pl.ds(pl.multiple_of(base + place * slab, slab), slab), :],
            keep_sem.at[a, slot],
        )

    def hand_on(a, slot, forward):
        dst = arrays[a][1]
        if forward:
            src_rows, dst_rows, target = pl.ds(2 * block_len, block_len), pl.ds(0, block_len), blk + 2
        else:
            src_rows, dst_rows, target = pl.ds(block_len, block_len), pl.ds(3 * block_len, block_len), blk - 2
        return pltpu.make_async_remote_copy(
            src_ref=dst.at[slot, src_rows, :],
            dst_ref=dst.at[slot, dst_rows, :],
            send_sem=pass_send.at[a, slot, forward],
            recv_sem=pass_recv.at[a, slot, forward],
            device_id=(target, part),
            device_id_type=MESH,
        )

    def start_all(a, slot):
        for i in range(len(offsets)):
            @pl.when(pushed_to(slot, i))
            def _(i=i):
                push(a, slot, i).start()

        @pl.when(held(own, slot))
        def _():
            keep(a, slot).start()

    def sent_all(a, slot):
        for i in range(len(offsets)):
            @pl.when(pushed_to(slot, i))
            def _(i=i):
                push(a, slot, i).wait_send()

    def arrive_all(a, slot):
        @pl.when(held(own, slot))
        def _():
            for i in range(len(offsets)):
                push(a, slot, i).wait_recv()
            keep(a, slot).wait()

    def hand_on_all(a, slot):
        @pl.when(held(own, slot) & has_prev)
        def _():
            hand_on(a, slot, 0).start()

        @pl.when(held(own, slot) & has_next)
        def _():
            hand_on(a, slot, 1).start()

    def handed_all(slot):
        for a in range(2):
            @pl.when(held(own, slot) & has_prev)
            def _(a=a):
                hand_on(a, slot, 1).wait_recv()

            @pl.when(held(own, slot) & has_next)
            def _(a=a):
                hand_on(a, slot, 0).wait_recv()

    def handed_away(slot):
        for a in range(2):
            @pl.when(held(own, slot) & has_prev)
            def _(a=a):
                hand_on(a, slot, 0).wait_send()

            @pl.when(held(own, slot) & has_next)
            def _(a=a):
                hand_on(a, slot, 1).wait_send()

    window = 2 * block_len + QUERY_TILE

    def attend(slot, block):
        per_block = block_len // QUERY_TILE
        part_rows = QUERY_TILE // MERGE

        @pl.loop(0, per_block)
        def _(n):
            begin = pl.multiple_of((block * per_block + n) * QUERY_TILE, QUERY_TILE)
            at = pl.ds(begin, QUERY_TILE)
            left = jnp.concatenate([queries[slot, at, :], query_marks[at, :]], axis=1)
            chunks = [pl.ds(pl.multiple_of(begin + c, QUERY_TILE), KEY_TILE) for c in range(0, window, KEY_TILE)]
            scores = [
                lax.dot_general(
                    left, jnp.concatenate([keys[slot, c, :], key_marks[c, :]], axis=1),
                    (((1,), (1,)), ((), ())), preferred_element_type=jnp.float32,
                )
                for c in chunks
            ]
            top = functools.reduce(jnp.maximum, [jnp.max(x, axis=1, keepdims=True) for x in scores])
            top = jnp.maximum(top, least_top)
            ones = jnp.ones((KEY_TILE, HEAD), jnp.bfloat16)
            mixed = jnp.zeros((QUERY_TILE, 2 * HEAD), jnp.float32)
            for x, c in zip(scores, chunks):
                terms = jnp.exp2((x - top) * score_scale).astype(jnp.bfloat16)
                right = jnp.concatenate([values_held[slot, c, :], ones], axis=1)
                mixed += jnp.dot(terms, right, preferred_element_type=jnp.float32)
            mixed_ref[...] = mixed[:, :HEAD] / jnp.maximum(mixed[:, HEAD:], 1.0)
            for r in range(MERGE):
                rows_to = pl.ds(pl.multiple_of(r * (block_len // MERGE) + n * part_rows, part_rows), part_rows)
                o_ref[slot, block, rows_to, :] = mixed_ref[
                    pl.ds(r, part_rows, stride=MERGE), :
                ].astype(jnp.bfloat16)

    slot_range, steps = range(slots), range(1, x_len)

    def send_own(slot):
        @pl.when(held(own, slot))
        def _():
            attend(slot, side)
            for d in steps:
                go_x(0, slot, d).start()
            go_c(0, slot).start()
            stay(slot).start()

    def send_far(slot):
        @pl.when(held(far, slot))
        def _():
            go_y(slot).wait_recv()
            for d in steps:
                go_x(1, slot, d).start()
            go_c(1, slot).start()

    def send_on(slot, kind):
        for d in steps:
            @pl.when(held(place_of(kind, lax.rem(place_x + x_len - d, x_len), core), slot))
            def _(d=d):
                go_x(kind, slot, d).wait_recv()
                go_f(kind, slot, d).start()

    for a in range(3):
        start_all(a, 0)
    load.start()

    lane_of_key = lax.broadcasted_iota(jnp.int32, (block_len, LANES), 1)
    for n in range(4):
        at = slice(n * block_len, (n + 1) * block_len)
        segs = seg_ref[at, :]
        marked = jnp.where(segs >= 0, segs, LANES - 1) == lane_of_key
        key_marks[at, :] = jnp.where(marked, 1.0, 0.0).astype(jnp.bfloat16)
        if n in (1, 2):
            query_marks[slice((n - 1) * block_len, n * block_len), :] = jnp.where(
                segs == lane_of_key, 0.0, masked_score
            ).astype(jnp.bfloat16)

    for slot in slot_range:
        for a in range(3):
            arrive_all(a, slot)
            if a < 2:
                hand_on_all(a, slot)
            if slot + 1 < slots:
                start_all(a, slot + 1)
        handed_all(slot)
        if slot > 0:
            send_far(slot - 1)

        @pl.when(held(own, slot))
        def _(slot=slot):
            attend(slot, 1 - side)
            go_y(slot).start()

        if slot > 0:
            for kind in range(2):
                send_on(slot - 1, kind)
        send_own(slot)
    send_far(slots - 1)
    for kind in range(2):
        send_on(slots - 1, kind)
    for slot in slot_range:
        for a in range(3):
            sent_all(a, slot)
        handed_away(slot)

    for slot in slot_range:
        @pl.when(held(own, slot))
        def _(slot=slot):
            stay(slot).wait()
            go_y(slot).wait_send()

        for kind in range(2):
            @pl.when(held(own if kind == 0 else far, slot))
            def _(kind=kind, slot=slot):
                for d in steps:
                    go_x(kind, slot, d).wait_send()
                go_c(kind, slot).wait_send()

            @pl.when(held(place_of(kind, place_x, 1 - core), slot))
            def _(kind=kind, slot=slot):
                go_c(kind, slot).wait_recv()

            for d in steps:
                from_x = lax.rem(place_x + x_len - d, x_len)

                @pl.when(held(place_of(kind, from_x, core), slot))
                def _(kind=kind, slot=slot, d=d):
                    go_f(kind, slot, d).wait_send()

                @pl.when(held(place_of(kind, from_x, 1 - core), slot))
                def _(kind=kind, slot=slot, d=d):
                    go_f(kind, slot, d).wait_recv()
    load.wait()

    rows = projected.shape[0]
    width = heads * HEAD

    def product(r):
        at = pl.ds(pl.multiple_of(r * rows, rows), rows)
        left = jnp.concatenate([merged[h, at, :] for h in range(heads)], axis=1)
        right = weight[pl.ds(pl.multiple_of(r * width, width), width), :]
        return jnp.dot(left, right, preferred_element_type=jnp.float32)

    projected[...] = product(0)

    @pl.loop(1, MERGE)
    def _(r):
        projected[...] += product(r)

    values = projected[...]
    lane = lax.broadcasted_iota(jnp.int32, (rows, LANES), 1)
    own_rows = pl.ds((1 + side) * block_len, rows, stride=MERGE)
    member = seg_ref[own_rows, :] == lane
    squares = jnp.sum(values * values, axis=1, keepdims=True)
    tops = jnp.max(values, axis=1, keepdims=True)
    sums = jnp.sum(jnp.where(member, squares, 0.0), axis=0, keepdims=True)
    peaks = jnp.max(jnp.where(member, tops, masked_score), axis=0, keepdims=True)
    counts = jnp.sum(member.astype(jnp.float32), axis=0, keepdims=True) * values.shape[1]
    line = lax.broadcasted_iota(jnp.int32, (8, LANES), 0)

    def spread(stats, tile, me, count, target_of, send, recv):
        stats[me] = tile

        def send_to(d):
            return pltpu.make_async_remote_copy(
                src_ref=stats.at[me], dst_ref=stats.at[me],
                send_sem=send.at[d - 1], recv_sem=recv.at[d - 1],
                device_id=target_of(d), device_id_type=MESH,
            )

        for d in range(1, count):
            send_to(d).start()
        for d in range(1, count):
            send_to(d).wait()
        every = stats[...]
        return jnp.where(line == 1, jnp.max(every, axis=0), jnp.sum(every, axis=0))

    tile = jnp.where(line == 0, sums, jnp.where(line == 1, peaks, counts))
    tile = spread(part_stats, tile, part, tp, lambda d: (blk, lax.rem(part + d, tp)), p_send, p_recv)
    tile = spread(blk_stats, tile, blk, blks, lambda d: (lax.rem(blk + d, blks), part), b_send, b_recv)
    scale = lax.rsqrt(tile[0:1] / jnp.maximum(tile[2:3], 1.0) + epsilon)
    row_scale = jnp.sum(jnp.where(member, scale, 0.0), axis=1, keepdims=True)
    normed_ref[...] = (values * row_scale).astype(jnp.bfloat16)
    peak_ref[...] = jnp.broadcast_to(tile[1:2] * scale, (8, LANES))


def per_device(queries, keys, values, segment_ids, proj_weight):
    blks, tp = lax.axis_size("blk"), lax.axis_size("tp")
    blk = lax.axis_index("blk")
    width = queries.shape[1]
    heads = width // HEAD
    block_len = segment_ids.shape[0] // blks
    places = 2 * tp
    slots = -(-heads // places)
    peers = places - 1
    pair_len = 2 * block_len
    columns = proj_weight.shape[1]
    dma, anywhere = pltpu.SemaphoreType.DMA, pl.BlockSpec(memory_space=pl.ANY)
    in_vmem = pl.BlockSpec(memory_space=pltpu.VMEM)
    edge = jnp.full((block_len,), -2, jnp.int32)
    pair_segs = lax.dynamic_slice_in_dim(
        jnp.concatenate([edge, segment_ids, edge]), (blk // 2) * pair_len, 2 * pair_len
    )
    x_len = tp // 2
    merged_rows = block_len // MERGE
    sems = [dma((3, slots, peers))] * 2 + [dma((3, slots))] + [dma((2, slots, 2))] * 2
    sems += [dma(()), dma((slots,)), dma((slots,)), dma((slots,))]
    sems += [dma((2, slots, x_len - 1))] * 2 + [dma((2, slots))] * 2 + [dma((2, slots, x_len - 1))] * 2
    sems += [dma((tp - 1,))] * 2 + [dma((blks - 1,))] * 2
    vmem16 = lambda *shape: pltpu.VMEM(shape, jnp.bfloat16)
    vmem32 = lambda *shape: pltpu.VMEM(shape, jnp.float32)
    normed, peaks = pl.pallas_call(
        functools.partial(whole_kernel, tp, blks, heads, slots, block_len),
        out_shape=[
            jax.ShapeDtypeStruct((merged_rows, columns), jnp.bfloat16),
            jax.ShapeDtypeStruct((8, LANES), jnp.float32),
        ],
        in_specs=[anywhere, anywhere, anywhere, in_vmem, anywhere],
        out_specs=[in_vmem, in_vmem],
        scratch_shapes=[
            vmem16(slots, pair_len, HEAD),
            vmem16(slots, 2 * pair_len, HEAD),
            vmem16(slots, 2 * pair_len, HEAD),
            vmem16(2 * pair_len, LANES),
            vmem16(pair_len, LANES),
            vmem16(slots, 2, block_len, HEAD),
            vmem32(QUERY_TILE, HEAD),
            vmem16(heads, block_len, HEAD),
            vmem16(*proj_weight.shape),
            vmem32(merged_rows, columns),
            vmem32(tp, 8, LANES),
            vmem32(blks, 8, LANES),
        ] + sems,
        compiler_params=pltpu.CompilerParams(
            collective_id=0, has_side_effects=True, vmem_limit_bytes=56 * 1024 * 1024
        ),
        name="whole",
    )(queries, keys, values, pair_segs[:, None], proj_weight)
    return normed, peaks[0, :blks]


def solution(mesh):
    in_specs = (
        P(("blk", "tp"), None),
        P(("blk", "tp"), None),
        P(("blk", "tp"), None),
        P(),
        P(None, "tp"),
    )
    out_specs = (P("blk", "tp"), P())
    return jax.shard_map(
        per_device, mesh=mesh, in_specs=in_specs, out_specs=out_specs, check_vma=False
    )
```

time: 513 us -> 96 us (0.19)
  waiting for transfers between devices: 306 us -> 0 us
  Pallas kernels: 0 us -> 89.4 us
  blocking collectives: 80.4 us -> 0 us
  matrix products: 49.8 us -> 0 us
  other arithmetic: 29.2 us -> 0.73 us
  local copies, waits for them, and re-layouts: 21.7 us -> 4.96 us
  between operations: 13.8 us -> 0.67 us
  starting transfers between devices: 11.4 us -> 0 us
    ppermute x4 -> x0, waiting for transfers between devices: 221 us -> none  [from_behind(): return lax.ppermute(x, axis, pairs)]
    pallas_call x0 -> x1, Pallas kernels: none -> 89.4 us  [per_device(): pl.pallas_call(functools.partial(whole_kernel, tp, blks, heads, slots, bl...]
    all_gather x3 -> x0, waiting for transfers between devices: 84.3 us -> none  [the longest x1 32.5 us: per_device(): lax.all_gather(keys, 'tp', axis=0, tiled=True)]
    pmax x1 -> x0, blocking collectives: 41 us -> none  [per_device(): row_peak = lax.pmax(row_peak, ('blk', 'tp'))]
    psum x1 -> x0, blocking collectives: 39.4 us -> none  [per_device(): seg_sums, seg_counts = lax.psum((seg_sums, seg_counts), ('blk', 'tp'))]
    sub x1 -> x0, matrix products: 29.4 us -> none  [finish(): exp_terms = jnp.where(allowed[None], jnp.exp(scores - row_top), 0.0)]
    concatenate x3 -> x1, other arithmetic: 25.2 us -> 0.73 us  [per_device(): jnp.concatenate([edge, segment_ids, edge])]
    dot_general x2 -> x0, matrix products: 20.4 us -> none  [the longest x1 12.5 us: finish(): jnp.einsum('hrk,khd->rhd', weights, value_heads, preferred_element_type=j...]
  transfers between devices with their start and end apart: 7 -> 0, of which waited for: 5 -> 0; matrix products, arithmetic and copies ran while one was open for 9% -> 0% of each run, Pallas kernels for 0% -> 0%
where the time goes in v2:
time: 96 us; the launch traced here: 95.8 us
  Pallas kernels  89.4 us (93%)
  local copies, waits for them, and re-layouts  4.96 us (5%)
    pallas_call x1, Pallas kernels, per_device(): pl.pallas_call(functools.partial(whole_kernel, tp, blks, heads, slots, bl...  89.4 us
    broadcast_in_dim x1, local copies, waits for them, and re-layouts, per_device(): pair_segs[:, None]  2 us

profile of v2, /device:TPU:0, one launch (start us, length us, event | category | flops | bytes accessed | tf_op | source)
XLA Modules:
  0.0 95.8 jit_solution(6819349135672288348)
XLA Ops:
  0.7 0.7 fusion.1
  1.4 2.0 %copy.7.seg_ref = s32[4096,1]{1,0:T(8,128)} copy(s32[4096,1]{0,1:T(1,128)S(1)} %bitcast.3) | data formatting | bytes 32768 | tf_op jit(solution)/shard_map/broadcast_in_dim | solution.py:441
  3.4 89.4 %whole.1 = (bf16[256,768]{1,0:T(8,128)(2,1)}, f32[8,128]{1,0:T(8,128)}) custom-call(bf16[256,1664]{1,0:T(8,128)(2,1)} %q_in.1, bf16[256,1664]{1,0:T(8,128)(2,1)} %k_in.1, bf16[256,1664]{1,0:T(8,128)(2,1)} %v_in.1, s32[4096,1]{1,0:T(8,128)} %copy.7.seg_ref, bf16[6656,768]{1,0:T(8,128)(2,1)} %w_ref.1), custom_call_target="tpu_custom_call" | custom-call | tf_op jit(solution)/shard_map/whole/pallas_call | solution.py:415
  92.8 1.2 %slice_bitcast_fusion = f32[8]{0:T(128)} fusion(f32[8,128]{1,0:T(8,128)} %get-tuple-element.5), kind=kLoop, calls=%fused_computation.5 | loop fusion | bytes 64 | tf_op jit(solution)/shard_map/squeeze | solution.py:442
  94.0 1.8 %copy.9 = bf16[256,768]{1,0:T(8,128)(2,1)} copy(bf16[256,768]{1,0:T(8,128)(2,1)} %get-tuple-element.8) | data formatting | bytes 786432
  (1 shorter events, 0.0 us)

commit v3 on v2

--- a/solution.py
+++ b/solution.py
@@ -11,6 +11,7 @@
 MERGE = 4
 QUERY_TILE = 256
 KEY_TILE = 768
+TOGETHER = 2
 LANES = 128
 masked_score = -1e30
 least_top = -1e20
@@ -26,7 +27,7 @@
 def whole_kernel(
     tp, blks, heads, slots, block_len,
     q_in, k_in, v_in, seg_ref, w_ref, normed_ref, peak_ref,
-    queries, keys, values_held, key_marks, query_marks, o_ref, mixed_ref,
+    queries, keys, values_held, key_marks, query_marks, row_marks, o_ref, mixed_ref,
     merged, weight, projected, part_stats, blk_stats,
     send, recv, keep_sem, pass_send, pass_recv,
     w_sem, own_sem, y_send, y_recv, x_send, x_recv, c_send, c_recv, f_send, f_recv,
@@ -209,33 +210,39 @@
         per_block = block_len // QUERY_TILE
         part_rows = QUERY_TILE // MERGE
 
-        @pl.loop(0, per_block)
-        def _(n):
-            begin = pl.multiple_of((block * per_block + n) * QUERY_TILE, QUERY_TILE)
-            at = pl.ds(begin, QUERY_TILE)
-            left = jnp.concatenate([queries[slot, at, :], query_marks[at, :]], axis=1)
-            chunks = [pl.ds(pl.multiple_of(begin + c, QUERY_TILE), KEY_TILE) for c in range(0, window, KEY_TILE)]
-            scores = [
-                lax.dot_general(
-                    left, jnp.concatenate([keys[slot, c, :], key_marks[c, :]], axis=1),
-                    (((1,), (1,)), ((), ())), preferred_element_type=jnp.float32,
-                )
-                for c in chunks
-            ]
-            top = functools.reduce(jnp.maximum, [jnp.max(x, axis=1, keepdims=True) for x in scores])
-            top = jnp.maximum(top, least_top)
+        @pl.loop(0, per_block // TOGETHER)
+        def _(step):
+            tiles = [step * TOGETHER + u for u in range(TOGETHER)]
+            at, chunks, scores = [], [], []
+            for n in tiles:
+                begin = pl.multiple_of((block * per_block + n) * QUERY_TILE, QUERY_TILE)
+                rows = pl.ds(begin, QUERY_TILE)
+                left = jnp.concatenate([queries[slot, rows, :], query_marks[rows, :]], axis=1)
+                mine = [pl.ds(pl.multiple_of(begin + c, QUERY_TILE), KEY_TILE) for c in range(0, window, KEY_TILE)]
+                chunks.append(mine)
+                scores.append([
+                    lax.dot_general(
+                        left, jnp.concatenate([keys[slot, c, :], key_marks[c, :]], axis=1),
+                        (((1,), (1,)), ((), ())), preferred_element_type=jnp.float32,
+                    )
+                    for c in mine
+                ])
             ones = jnp.ones((KEY_TILE, HEAD), jnp.bfloat16)
-            mixed = jnp.zeros((QUERY_TILE, 2 * HEAD), jnp.float32)
-            for x, c in zip(scores, chunks):
-                terms = jnp.exp2((x - top) * score_scale).astype(jnp.bfloat16)
-                right = jnp.concatenate([values_held[slot, c, :], ones], axis=1)
-                mixed += jnp.dot(terms, right, preferred_element_type=jnp.float32)
-            mixed_ref[...] = mixed[:, :HEAD] / jnp.maximum(mixed[:, HEAD:], 1.0)
-            for r in range(MERGE):
-                rows_to = pl.ds(pl.multiple_of(r * (block_len // MERGE) + n * part_rows, part_rows), part_rows)
-                o_ref[slot, block, rows_to, :] = mixed_ref[
-                    pl.ds(r, part_rows, stride=MERGE), :
-                ].astype(jnp.bfloat16)
+            for u, n in enumerate(tiles):
+                top = functools.reduce(jnp.maximum, [jnp.max(x, axis=1, keepdims=True) for x in scores[u]])
+                top = jnp.maximum(top, least_top)
+                mixed = jnp.zeros((QUERY_TILE, 2 * HEAD), jnp.float32)
+                for x, c in zip(scores[u], chunks[u]):
+                    terms = jnp.exp2((x - top) * score_scale).astype(jnp.bfloat16)
+                    right = jnp.concatenate([values_held[slot, c, :], ones], axis=1)
+                    mixed += jnp.dot(terms, right, preferred_element_type=jnp.float32)
+                mixed_ref[u] = mixed[:, :HEAD] / jnp.maximum(mixed[:, HEAD:], 1.0)
+            for u, n in enumerate(tiles):
+                for r in range(MERGE):
+                    rows_to = pl.ds(pl.multiple_of(r * (block_len // MERGE) + n * part_rows, part_rows), part_rows)
+                    o_ref[slot, block, rows_to, :] = mixed_ref[
+                        u, pl.ds(r, part_rows, stride=MERGE), :
+                    ].astype(jnp.bfloat16)
 
     slot_range, steps = range(slots), range(1, x_len)
 
@@ -267,16 +274,22 @@
         start_all(a, 0)
     load.start()
 
-    lane_of_key = lax.broadcasted_iota(jnp.int32, (block_len, LANES), 1)
+    image = lax.broadcasted_iota(jnp.int32, (LANES, block_len), 0)
+    lane = lax.broadcasted_iota(jnp.int32, (block_len, LANES), 1)
     for n in range(4):
-        at = slice(n * block_len, (n + 1) * block_len)
-        segs = seg_ref[at, :]
-        marked = jnp.where(segs >= 0, segs, LANES - 1) == lane_of_key
-        key_marks[at, :] = jnp.where(marked, 1.0, 0.0).astype(jnp.bfloat16)
+        block = pair * 2 - 1 + n
+        inside = (block >= 0) & (block < blks)
+        from_row = jnp.clip(block, 0, blks - 1) * block_len
+        segs = seg_ref[:, pl.ds(pl.multiple_of(from_row, LANES), block_len)]
+        segs = jnp.where(inside & (segs >= 0), segs, LANES - 1)
+        marks = jnp.where(segs == image, 1.0, 0.0).T
+        key_marks[n * block_len : (n + 1) * block_len, :] = marks.astype(jnp.bfloat16)
         if n in (1, 2):
-            query_marks[slice((n - 1) * block_len, n * block_len), :] = jnp.where(
-                segs == lane_of_key, 0.0, masked_score
+            query_marks[(n - 1) * block_len : n * block_len, :] = jnp.where(
+                (marks > 0.5) & (lane < LANES - 1), 0.0, masked_score
             ).astype(jnp.bfloat16)
+            row_marks[n - 1] = marks
+    projected[...] = jnp.zeros_like(projected)
 
     for slot in slot_range:
         for a in range(3):
@@ -298,62 +311,77 @@
             for kind in range(2):
                 send_on(slot - 1, kind)
         send_own(slot)
+    def gathered(slot):
+        @pl.when(held(own, slot))
+        def _():
+            stay(slot).wait()
+
+        for kind in range(2):
+            @pl.when(held(place_of(kind, place_x, 1 - core), slot))
+            def _(kind=kind):
+                go_c(kind, slot).wait_recv()
+
+            for d in steps:
+                from_x = lax.rem(place_x + x_len - d, x_len)
+
+                @pl.when(held(place_of(kind, from_x, 1 - core), slot))
+                def _(kind=kind, d=d):
+                    go_f(kind, slot, d).wait_recv()
+
+    def let_go(slot):
+        @pl.when(held(own, slot))
+        def _():
+            go_y(slot).wait_send()
+
+        for kind in range(2):
+            @pl.when(held(own if kind == 0 else far, slot))
+            def _(kind=kind):
+                for d in steps:
+                    go_x(kind, slot, d).wait_send()
+                go_c(kind, slot).wait_send()
+
+            for d in steps:
+                @pl.when(held(place_of(kind, lax.rem(place_x + x_len - d, x_len), core), slot))
+                def _(kind=kind, d=d):
+                    go_f(kind, slot, d).wait_send()
+
+    rows = projected.shape[0]
+    width = heads * HEAD
+
+    def product(slot):
+        present = [
+            start_head(g, places, heads) + slot
+            for g in range(places)
+            if slot < start_head(g + 1, places, heads) - start_head(g, places, heads)
+        ]
+
+        @pl.loop(0, MERGE)
+        def _(r):
+            at = pl.ds(pl.multiple_of(r * rows, rows), rows)
+            left = jnp.concatenate([merged[h, at, :] for h in present], axis=1)
+            right = jnp.concatenate(
+                [weight[pl.ds(pl.multiple_of(r * width + h * HEAD, HEAD), HEAD), :] for h in present], axis=0
+            )
+            projected[...] += jnp.dot(left, right, preferred_element_type=jnp.float32)
+
     send_far(slots - 1)
+    load.wait()
+    for slot in range(slots - 1):
+        gathered(slot)
+        product(slot)
     for kind in range(2):
         send_on(slots - 1, kind)
+    gathered(slots - 1)
+    product(slots - 1)
     for slot in slot_range:
         for a in range(3):
             sent_all(a, slot)
         handed_away(slot)
-
-    for slot in slot_range:
-        @pl.when(held(own, slot))
-        def _(slot=slot):
-            stay(slot).wait()
-            go_y(slot).wait_send()
-
-        for kind in range(2):
-            @pl.when(held(own if kind == 0 else far, slot))
-            def _(kind=kind, slot=slot):
-                for d in steps:
-                    go_x(kind, slot, d).wait_send()
-                go_c(kind, slot).wait_send()
-
-            @pl.when(held(place_of(kind, place_x, 1 - core), slot))
-            def _(kind=kind, slot=slot):
-                go_c(kind, slot).wait_recv()
-
-            for d in steps:
-                from_x = lax.rem(place_x + x_len - d, x_len)
-
-                @pl.when(held(place_of(kind, from_x, core), slot))
-                def _(kind=kind, slot=slot, d=d):
-                    go_f(kind, slot, d).wait_send()
-
-                @pl.when(held(place_of(kind, from_x, 1 - core), slot))
-                def _(kind=kind, slot=slot, d=d):
-                    go_f(kind, slot, d).wait_recv()
-    load.wait()
-
-    rows = projected.shape[0]
-    width = heads * HEAD
-
-    def product(r):
-        at = pl.ds(pl.multiple_of(r * rows, rows), rows)
-        left = jnp.concatenate([merged[h, at, :] for h in range(heads)], axis=1)
-        right = weight[pl.ds(pl.multiple_of(r * width, width), width), :]
-        return jnp.dot(left, right, preferred_element_type=jnp.float32)
-
-    projected[...] = product(0)
-
-    @pl.loop(1, MERGE)
-    def _(r):
-        projected[...] += product(r)
+        let_go(slot)
 
     values = projected[...]
     lane = lax.broadcasted_iota(jnp.int32, (rows, LANES), 1)
-    own_rows = pl.ds((1 + side) * block_len, rows, stride=MERGE)
-    member = seg_ref[own_rows, :] == lane
+    member = (row_marks[side, pl.ds(0, rows, stride=MERGE), :] > 0.5) & (lane < LANES - 1)
     squares = jnp.sum(values * values, axis=1, keepdims=True)
     tops = jnp.max(values, axis=1, keepdims=True)
     sums = jnp.sum(jnp.where(member, squares, 0.0), axis=0, keepdims=True)
@@ -384,12 +412,11 @@
     scale = lax.rsqrt(tile[0:1] / jnp.maximum(tile[2:3], 1.0) + epsilon)
     row_scale = jnp.sum(jnp.where(member, scale, 0.0), axis=1, keepdims=True)
     normed_ref[...] = (values * row_scale).astype(jnp.bfloat16)
-    peak_ref[...] = jnp.broadcast_to(tile[1:2] * scale, (8, LANES))
+    peak_ref[...] = (tile[1:2] * scale)[0, :blks]
 
 
 def per_device(queries, keys, values, segment_ids, proj_weight):
     blks, tp = lax.axis_size("blk"), lax.axis_size("tp")
-    blk = lax.axis_index("blk")
     width = queries.shape[1]
     heads = width // HEAD
     block_len = segment_ids.shape[0] // blks
@@ -400,10 +427,6 @@
     columns = proj_weight.shape[1]
     dma, anywhere = pltpu.SemaphoreType.DMA, pl.BlockSpec(memory_space=pl.ANY)
     in_vmem = pl.BlockSpec(memory_space=pltpu.VMEM)
-    edge = jnp.full((block_len,), -2, jnp.int32)
-    pair_segs = lax.dynamic_slice_in_dim(
-        jnp.concatenate([edge, segment_ids, edge]), (blk // 2) * pair_len, 2 * pair_len
-    )
     x_len = tp // 2
     merged_rows = block_len // MERGE
     sems = [dma((3, slots, peers))] * 2 + [dma((3, slots))] + [dma((2, slots, 2))] * 2
@@ -416,7 +439,7 @@
         functools.partial(whole_kernel, tp, blks, heads, slots, block_len),
         out_shape=[
             jax.ShapeDtypeStruct((merged_rows, columns), jnp.bfloat16),
-            jax.ShapeDtypeStruct((8, LANES), jnp.float32),
+            jax.ShapeDtypeStruct((blks,), jnp.float32),
         ],
         in_specs=[anywhere, anywhere, anywhere, in_vmem, anywhere],
         out_specs=[in_vmem, in_vmem],
@@ -426,8 +449,9 @@
             vmem16(slots, 2 * pair_len, HEAD),
             vmem16(2 * pair_len, LANES),
             vmem16(pair_len, LANES),
+            vmem32(2, block_len, LANES),
             vmem16(slots, 2, block_len, HEAD),
-            vmem32(QUERY_TILE, HEAD),
+            vmem32(TOGETHER, QUERY_TILE, HEAD),
             vmem16(heads, block_len, HEAD),
             vmem16(*proj_weight.shape),
             vmem32(merged_rows, columns),
@@ -438,8 +462,8 @@
             collective_id=0, has_side_effects=True, vmem_limit_bytes=56 * 1024 * 1024
         ),
         name="whole",
-    )(queries, keys, values, pair_segs[:, None], proj_weight)
-    return normed, peaks[0, :blks]
+    )(queries, keys, values, segment_ids[None], proj_weight)
+    return normed, peaks
 
 
 def solution(mesh):

time: 96 us -> 80 us (0.83)
  Pallas kernels: 89.4 us -> 76.2 us
  local copies, waits for them, and re-layouts: 4.96 us -> 2.89 us
    pallas_call x1, Pallas kernels: 89.4 us -> 76.2 us  [per_device(): pl.pallas_call(functools.partial(whole_kernel, tp, blks, heads, slots, bl...]
    broadcast_in_dim x2 -> x0, local copies, waits for them, and re-layouts: 2 us -> none  [the longest x1 2 us: per_device(): pair_segs[:, None]]
    squeeze x1 -> x0, local copies, waits for them, and re-layouts: 1.19 us -> none  [per_device(): return (normed, peaks[0, :blks])]
    unnamed x1 -> x2, local copies, waits for them, and re-layouts: 1.77 us -> 2.89 us
where the time goes in v3:
time: 80 us; the launch traced here: 79.8 us
  Pallas kernels  76.2 us (95%)
  local copies, waits for them, and re-layouts  2.89 us (4%)
    pallas_call x1, Pallas kernels, per_device(): pl.pallas_call(functools.partial(whole_kernel, tp, blks, heads, slots, bl...  76.2 us
    unnamed x2, local copies, waits for them, and re-layouts  2.89 us

profile of v3, /device:TPU:0, one launch (start us, length us, event | category | flops | bytes accessed | tf_op | source)
XLA Modules:
  0.0 79.8 jit_solution(17465006779336487632)
XLA Ops:
  0.6 76.2 %whole.1 = (bf16[256,768]{1,0:T(8,128)(2,1)}, f32[8]{0:T(128)}) custom-call(bf16[256,1664]{1,0:T(8,128)(2,1)} %q_in.1, bf16[256,1664]{1,0:T(8,128)(2,1)} %k_in.1, bf16[256,1664]{1,0:T(8,128)(2,1)} %v_in.1, s32[1,8192]{1,0:T(1,128)} %bitcast.1, bf16[6656,768]{1,0:T(8,128)(2,1)} %w_ref.1), custom_call_target="tpu_custom_call" | custom-call | tf_op jit(solution)/shard_map/whole/pallas_call | solution.py:438
  76.9 1.8 %copy.9 = bf16[256,768]{1,0:T(8,128)(2,1)} copy(bf16[256,768]{1,0:T(8,128)(2,1)} %get-tuple-element.4) | data formatting | bytes 786432
  78.6 1.1 %copy.10 = f32[8]{0:T(128)} copy(f32[8]{0:T(128)} %get-tuple-element.5) | data formatting | bytes 64

commit v4 on v3

--- a/solution.py
+++ b/solution.py
@@ -11,7 +11,7 @@
 MERGE = 4
 QUERY_TILE = 256
 KEY_TILE = 768
-TOGETHER = 2
+TOGETHER = 4
 LANES = 128
 masked_score = -1e30
 least_top = -1e20
@@ -213,30 +213,42 @@
         @pl.loop(0, per_block // TOGETHER)
         def _(step):
             tiles = [step * TOGETHER + u for u in range(TOGETHER)]
-            at, chunks, scores = [], [], []
-            for n in tiles:
+            ones = jnp.ones((KEY_TILE, HEAD), jnp.bfloat16)
+
+            def parts_of(n):
                 begin = pl.multiple_of((block * per_block + n) * QUERY_TILE, QUERY_TILE)
+                return begin, [
+                    pl.ds(pl.multiple_of(begin + c, QUERY_TILE), KEY_TILE) for c in range(0, window, KEY_TILE)
+                ]
+
+            def score(n):
+                begin, chunks = parts_of(n)
                 rows = pl.ds(begin, QUERY_TILE)
                 left = jnp.concatenate([queries[slot, rows, :], query_marks[rows, :]], axis=1)
-                mine = [pl.ds(pl.multiple_of(begin + c, QUERY_TILE), KEY_TILE) for c in range(0, window, KEY_TILE)]
-                chunks.append(mine)
-                scores.append([
+                return [
                     lax.dot_general(
                         left, jnp.concatenate([keys[slot, c, :], key_marks[c, :]], axis=1),
                         (((1,), (1,)), ((), ())), preferred_element_type=jnp.float32,
                     )
-                    for c in mine
-                ])
-            ones = jnp.ones((KEY_TILE, HEAD), jnp.bfloat16)
-            for u, n in enumerate(tiles):
-                top = functools.reduce(jnp.maximum, [jnp.max(x, axis=1, keepdims=True) for x in scores[u]])
+                    for c in chunks
+                ]
+
+            def mix(u, n, scores):
+                top = functools.reduce(jnp.maximum, [jnp.max(x, axis=1, keepdims=True) for x in scores])
                 top = jnp.maximum(top, least_top)
                 mixed = jnp.zeros((QUERY_TILE, 2 * HEAD), jnp.float32)
-                for x, c in zip(scores[u], chunks[u]):
+                for x, c in zip(scores, parts_of(n)[1]):
                     terms = jnp.exp2((x - top) * score_scale).astype(jnp.bfloat16)
                     right = jnp.concatenate([values_held[slot, c, :], ones], axis=1)
                     mixed += jnp.dot(terms, right, preferred_element_type=jnp.float32)
                 mixed_ref[u] = mixed[:, :HEAD] / jnp.maximum(mixed[:, HEAD:], 1.0)
+
+            ahead = score(tiles[0])
+            for u, n in enumerate(tiles):
+                scores = ahead
+                if u + 1 < TOGETHER:
+                    ahead = score(tiles[u + 1])
+                mix(u, n, scores)
             for u, n in enumerate(tiles):
                 for r in range(MERGE):
                     rows_to = pl.ds(pl.multiple_of(r * (block_len // MERGE) + n * part_rows, part_rows), part_rows)
@@ -270,8 +282,8 @@
                 go_x(kind, slot, d).wait_recv()
                 go_f(kind, slot, d).start()
 
-    for a in range(3):
-        start_all(a, 0)
+    start_all(0, 0)
+    start_all(1, 0)
     load.start()
 
     image = lax.broadcasted_iota(jnp.int32, (LANES, block_len), 0)
@@ -291,26 +303,39 @@
             row_marks[n - 1] = marks
     projected[...] = jnp.zeros_like(projected)
 
+    def arrive_and_hand_on(a, slot):
+        arrive_all(a, slot)
+        hand_on_all(a, slot)
+
+    arrive_and_hand_on(0, 0)
+    start_all(2, 0)
+    arrive_and_hand_on(1, 0)
     for slot in slot_range:
-        for a in range(3):
-            arrive_all(a, slot)
-            if a < 2:
-                hand_on_all(a, slot)
-            if slot + 1 < slots:
-                start_all(a, slot + 1)
+        more = slot + 1 < slots
+        if more:
+            start_all(0, slot + 1)
+            start_all(1, slot + 1)
+        arrive_all(2, slot)
+        if more:
+            start_all(2, slot + 1)
         handed_all(slot)
-        if slot > 0:
-            send_far(slot - 1)
+        if more:
+            arrive_and_hand_on(0, slot + 1)
 
         @pl.when(held(own, slot))
         def _(slot=slot):
             attend(slot, 1 - side)
             go_y(slot).start()
 
+        if more:
+            arrive_and_hand_on(1, slot + 1)
         if slot > 0:
             for kind in range(2):
                 send_on(slot - 1, kind)
         send_own(slot)
+        if more:
+            send_far(slot)
+
     def gathered(slot):
         @pl.when(held(own, slot))
         def _():

time: 80 us -> 79.9 us (level)
  no operation moved by 1% of the time
where the time goes in v4:
time: 79.9 us; the launch traced here: 79.6 us
  Pallas kernels  76.1 us (95%)
  local copies, waits for them, and re-layouts  2.89 us (4%)
    pallas_call x1, Pallas kernels, per_device(): pl.pallas_call(functools.partial(whole_kernel, tp, blks, heads, slots, bl...  76.1 us
    unnamed x2, local copies, waits for them, and re-layouts  2.89 us

profile of v4, /device:TPU:0, one launch (start us, length us, event | category | flops | bytes accessed | tf_op | source)
XLA Modules:
  0.0 79.6 jit_solution(16694093668370391784)
XLA Ops:
  0.6 76.1 %whole.1 = (bf16[256,768]{1,0:T(8,128)(2,1)}, f32[8]{0:T(128)}) custom-call(bf16[256,1664]{1,0:T(8,128)(2,1)} %q_in.1, bf16[256,1664]{1,0:T(8,128)(2,1)} %k_in.1, bf16[256,1664]{1,0:T(8,128)(2,1)} %v_in.1, s32[1,8192]{1,0:T(1,128)} %bitcast.1, bf16[6656,768]{1,0:T(8,128)(2,1)} %w_ref.1), custom_call_target="tpu_custom_call" | custom-call | tf_op jit(solution)/shard_map/whole/pallas_call | solution.py:463
  76.7 1.8 %copy.9 = bf16[256,768]{1,0:T(8,128)(2,1)} copy(bf16[256,768]{1,0:T(8,128)(2,1)} %get-tuple-element.4) | data formatting | bytes 786432
  78.5 1.1 %copy.10 = f32[8]{0:T(128)} copy(f32[8]{0:T(128)} %get-tuple-element.5) | data formatting | bytes 64

commit v5 on v4

--- a/solution.py
+++ b/solution.py
@@ -11,7 +11,7 @@
 MERGE = 4
 QUERY_TILE = 256
 KEY_TILE = 768
-TOGETHER = 4
+TOGETHER = 2
 LANES = 128
 masked_score = -1e30
 least_top = -1e20
@@ -261,7 +261,6 @@
     def send_own(slot):
         @pl.when(held(own, slot))
         def _():
-            attend(slot, side)
             for d in steps:
                 go_x(0, slot, d).start()
             go_c(0, slot).start()
@@ -310,31 +309,43 @@
     arrive_and_hand_on(0, 0)
     start_all(2, 0)
     arrive_and_hand_on(1, 0)
-    for slot in slot_range:
-        more = slot + 1 < slots
-        if more:
-            start_all(0, slot + 1)
-            start_all(1, slot + 1)
-        arrive_all(2, slot)
-        if more:
-            start_all(2, slot + 1)
-        handed_all(slot)
-        if more:
-            arrive_and_hand_on(0, slot + 1)
-
-        @pl.when(held(own, slot))
-        def _(slot=slot):
-            attend(slot, 1 - side)
+    if slots > 1:
+        start_all(0, 1)
+        start_all(1, 1)
+    arrive_all(2, 0)
+    if slots > 1:
+        start_all(2, 1)
+    handed_all(0)
+    if slots > 1:
+        arrive_and_hand_on(0, 1)
+
+    def after_far(slot):
+        @pl.when(held(own, slot))
+        def _():
             go_y(slot).start()
 
-        if more:
+        if slot + 1 < slots:
             arrive_and_hand_on(1, slot + 1)
         if slot > 0:
-            for kind in range(2):
-                send_on(slot - 1, kind)
+            send_far(slot - 1)
+
+    def after_own(slot):
         send_own(slot)
-        if more:
-            send_far(slot)
+        if slot + 1 < slots:
+            arrive_all(2, slot + 1)
+            handed_all(slot + 1)
+
+    @pl.loop(0, 2 * slots)
+    def _(phase):
+        slot = phase // 2
+
+        @pl.when(held(own, slot))
+        def _():
+            attend(slot, lax.rem(phase + 1 + side, 2))
+
+        for done in slot_range:
+            pl.when(phase == 2 * done)(functools.partial(after_far, done))
+            pl.when(phase == 2 * done + 1)(functools.partial(after_own, done))
 
     def gathered(slot):
         @pl.when(held(own, slot))
@@ -392,6 +403,8 @@
     send_far(slots - 1)
     load.wait()
     for slot in range(slots - 1):
+        for kind in range(2):
+            send_on(slot, kind)
         gathered(slot)
         product(slot)
     for kind in range(2):

time: 79.9 us -> 82 us (1.026)
  Pallas kernels: 76.1 us -> 78.2 us
    pallas_call x1, Pallas kernels: 76.1 us -> 78.2 us  [per_device(): pl.pallas_call(functools.partial(whole_kernel, tp, blks, heads, slots, bl...]
where the time goes in v5:
time: 82 us; the launch traced here: 81.7 us
  Pallas kernels  78.2 us (95%)
  local copies, waits for them, and re-layouts  2.89 us (4%)
    pallas_call x1, Pallas kernels, per_device(): pl.pallas_call(functools.partial(whole_kernel, tp, blks, heads, slots, bl...  78.2 us
    unnamed x2, local copies, waits for them, and re-layouts  2.89 us

profile of v5, /device:TPU:0, one launch (start us, length us, event | category | flops | bytes accessed | tf_op | source)
XLA Modules:
  0.0 81.7 jit_solution(15274882422685774895)
XLA Ops:
  0.6 78.2 %whole.1 = (bf16[256,768]{1,0:T(8,128)(2,1)}, f32[8]{0:T(128)}) custom-call(bf16[256,1664]{1,0:T(8,128)(2,1)} %q_in.1, bf16[256,1664]{1,0:T(8,128)(2,1)} %k_in.1, bf16[256,1664]{1,0:T(8,128)(2,1)} %v_in.1, s32[1,8192]{1,0:T(1,128)} %bitcast.1, bf16[6656,768]{1,0:T(8,128)(2,1)} %w_ref.1), custom_call_target="tpu_custom_call" | custom-call | tf_op jit(solution)/shard_map/whole/pallas_call | solution.py:476
  78.9 1.8 %copy.9 = bf16[256,768]{1,0:T(8,128)(2,1)} copy(bf16[256,768]{1,0:T(8,128)(2,1)} %get-tuple-element.4) | data formatting | bytes 786432
  80.6 1.1 %copy.10 = f32[8]{0:T(128)} copy(f32[8]{0:T(128)} %get-tuple-element.5) | data formatting | bytes 64

commit v6 on v3

--- a/solution.py
+++ b/solution.py
@@ -441,7 +441,7 @@
             jax.ShapeDtypeStruct((merged_rows, columns), jnp.bfloat16),
             jax.ShapeDtypeStruct((blks,), jnp.float32),
         ],
-        in_specs=[anywhere, anywhere, anywhere, in_vmem, anywhere],
+        in_specs=[in_vmem, in_vmem, in_vmem, in_vmem, anywhere],
         out_specs=[in_vmem, in_vmem],
         scratch_shapes=[
             vmem16(slots, pair_len, HEAD),

time: 80 us -> 80.7 us (level)
  no operation moved by 1% of the time
where the time goes in v6:
time: 80.7 us; the launch traced here: 80.5 us
  Pallas kernels  77 us (95%)
  local copies, waits for them, and re-layouts  2.89 us (4%)
    pallas_call x1, Pallas kernels, per_device(): pl.pallas_call(functools.partial(whole_kernel, tp, blks, heads, slots, bl...  77 us
    unnamed x2, local copies, waits for them, and re-layouts  2.89 us

profile of v6, /device:TPU:0, one launch (start us, length us, event | category | flops | bytes accessed | tf_op | source)
XLA Modules:
  0.0 80.5 jit_solution(11997561873890385195)
XLA Ops:
  0.6 77.0 %whole.1 = (bf16[256,768]{1,0:T(8,128)(2,1)}, f32[8]{0:T(128)}) custom-call(bf16[256,1664]{1,0:T(8,128)(2,1)} %q_in.1, bf16[256,1664]{1,0:T(8,128)(2,1)} %k_in.1, bf16[256,1664]{1,0:T(8,128)(2,1)} %v_in.1, s32[1,8192]{1,0:T(1,128)} %bitcast.1, bf16[6656,768]{1,0:T(8,128)(2,1)} %w_ref.1), custom_call_target="tpu_custom_call" | custom-call | tf_op jit(solution)/shard_map/whole/pallas_call | solution.py:438
  77.6 1.8 %copy.9 = bf16[256,768]{1,0:T(8,128)(2,1)} copy(bf16[256,768]{1,0:T(8,128)(2,1)} %get-tuple-element.4) | data formatting | bytes 786432
  79.4 1.1 %copy.10 = f32[8]{0:T(128)} copy(f32[8]{0:T(128)} %get-tuple-element.5) | data formatting | bytes 64
